TPU v7x, 768 devices: a whole 4x8x12 slice. The times are simulated.
768 devices in a mesh: seq: 48 (over x, z_lo, core), mp: 16 (over z_hi, y).
Axes of the slice: x: 4, y: 8, z: 12 (z_hi: 2, z_lo: 6; z = z_hi * 6 + z_lo), core: 2. Of those that a mesh axis runs over, the one named last changes fastest.
Arguments:
- vit_hidden: bfloat16 [12288, 3200], P('seq'), may hold values from -6 to 6
- vit_gain: float32 [3200], replicated, may hold values from 0.5 to 1.5
- vit_bias: float32 [3200], replicated, may hold values from -3 to 3
- proj_weight: bfloat16 [3200, 8192], P(None, 'mp'), may hold values from -0.109375 to 0.109375
- text_emb: bfloat16 [24576, 8192], P('seq', 'mp'), may hold values from -40 to 40
- llm_gain: float32 [8192], P('mp'), may hold values from 0.5 to 1.5
- cotangent: bfloat16 [24576, 8192], P('seq', 'mp'), may hold values from -6 to 6
- tile_start: int32 [48], replicated, may hold values from 0 to 3040, as said below
- tile_owner: int32 [48], replicated, may hold values from 0 to 47, each once
Outputs:
- normed: bfloat16 [24576, 8192], P('seq', 'mp')
- grad_text: bfloat16 [24576, 8192], P('seq', 'mp')
- grad_vit: bfloat16 [12288, 3200], P('seq', 'mp')
Inputs may be any that keep to these rules, and one draw needn't show every extreme that they name: `tile_start`: starts increase with the tile's index and tiles never intersect; tile 0 begins the packed stretch and the last tile ends it.
All inputs are finite; a program needn't handle non-finite values.
Results may differ from a plain program's by a relative error of at most 0.0015.
The roundings to bfloat16 on the way count: a program that leaves them out, or rounds other values in their place, can miss the bound.
Values may be sent and summed in bfloat16 or wider, within the bound.
A program may use at most 32 MiB of HBM per device.

v0:
```python
import jax
import jax.numpy as jnp
from jax import lax
from jax.sharding import PartitionSpec as P

D = 8192
BLK = 8
TILE_BLOCKS = 32


EPSILON = 1e-05


def unit_scale(hidden):
    values = hidden.astype(jnp.float32)
    centred = values - jnp.mean(values, axis=1, keepdims=True)
    inv_std = lax.rsqrt(jnp.mean(centred * centred, axis=1, keepdims=True) + EPSILON)
    return (centred * inv_std, inv_std)


def block_lookup(tile_start, tile_owner, global_block):
    started = (tile_start[None, :] <= global_block[:, None]).astype(jnp.int32)
    found = jnp.sum(started, axis=1) - 1
    tile_index = jnp.maximum(found, 0)
    offset = global_block - jnp.take(tile_start, tile_index)
    inside = (found >= 0) & (offset < TILE_BLOCKS)
    owner = jnp.take(tile_owner, tile_index)
    return (inside, owner, offset)


def body(
    vit_hidden,
    vit_gain,
    vit_bias,
    proj_weight,
    text_emb,
    llm_gain,
    cotangent,
    tile_start,
    tile_owner,
):
    ranks = lax.axis_size("seq")
    own_index = lax.axis_index("seq")
    slots = -(-TILE_BLOCKS // ranks)
    width = proj_weight.shape[1]
    tiles = tile_start.shape[0]
    local_blocks = text_emb.shape[0] // BLK
    unit_rows, inv_std = unit_scale(vit_hidden)
    normed_vit = (unit_rows * vit_gain + vit_bias).astype(jnp.bfloat16)
    image_embed = jnp.dot(normed_vit, proj_weight, preferred_element_type=jnp.float32).astype(
        jnp.bfloat16
    )
    embed_blocks = image_embed.reshape(TILE_BLOCKS, BLK, width)
    own_tile = jnp.sum(jnp.where(tile_owner == own_index, jnp.arange(tiles, dtype=jnp.int32), 0))
    own_start = jnp.take(tile_start, own_tile)
    target = jnp.arange(ranks, dtype=jnp.int32)[:, None]
    slot_ids = jnp.arange(slots, dtype=jnp.int32)[None, :]
    tile_block = ((target - own_start) % ranks + slot_ids * ranks).reshape(-1)
    placed = tile_block < TILE_BLOCKS
    outgoing = jnp.take(embed_blocks, jnp.minimum(tile_block, TILE_BLOCKS - 1), axis=0)
    outgoing = jnp.where(placed[:, None, None], outgoing, jnp.zeros_like(outgoing))
    incoming = lax.all_to_all(outgoing, "seq", split_axis=0, concat_axis=0, tiled=True)
    global_block = jnp.arange(local_blocks, dtype=jnp.int32) * ranks + own_index
    inside, owner, offset = block_lookup(tile_start, tile_owner, global_block)
    source_slot = jnp.where(inside, owner * slots + offset // ranks, 0)
    arriving = jnp.take(incoming, source_slot, axis=0)
    text_blocks = text_emb.reshape(local_blocks, BLK, width)
    merged = jnp.where(inside[:, None, None], arriving, text_blocks).reshape(-1, width)
    merged_f = merged.astype(jnp.float32)
    grad_gain = llm_gain * cotangent.astype(jnp.float32)
    squares, products = lax.psum(
        (jnp.sum(merged_f * merged_f, axis=1), jnp.sum(grad_gain * merged_f, axis=1)), "mp"
    )
    inv_rms = lax.rsqrt(squares / D + EPSILON)
    normed = (merged_f * inv_rms[:, None] * llm_gain).astype(jnp.bfloat16)
    grad_merged = (
        inv_rms[:, None] * grad_gain
        - merged_f * (inv_rms * inv_rms * inv_rms * products / D)[:, None]
    )
    image_rows = jnp.repeat(inside, BLK)
    grad_text = jnp.where(image_rows[:, None], 0.0, grad_merged).astype(jnp.bfloat16)
    grad_blocks = grad_merged.astype(jnp.bfloat16).reshape(local_blocks, BLK * width)
    slot_range = jnp.arange(ranks * slots, dtype=jnp.int32)
    selector = ((slot_range[:, None] == source_slot[None, :]) & inside[None, :]).astype(
        jnp.bfloat16
    )
    returning = jnp.dot(selector, grad_blocks, preferred_element_type=jnp.float32).astype(
        jnp.bfloat16
    )
    returning = returning.reshape(ranks, slots * BLK, width)
    returned = lax.all_to_all(returning, "seq", split_axis=0, concat_axis=0, tiled=True)
    tile_offsets = jnp.arange(TILE_BLOCKS, dtype=jnp.int32)
    back_index = (own_start + tile_offsets) % ranks * slots + tile_offsets // ranks
    grad_embed = jnp.take(returned, back_index, axis=0).reshape(-1, width)
    partial_grad = jnp.einsum(
        "rk,vk->rv", grad_embed, proj_weight, preferred_element_type=jnp.float32
    )
    share = lax.psum_scatter(partial_grad, "mp", scatter_dimension=1, tiled=True)
    share_width = share.shape[1]
    column_start = lax.axis_index("mp") * share_width
    full_grad = lax.all_gather(share, "mp", axis=1, tiled=True)
    scaled = full_grad * vit_gain
    first = jnp.mean(scaled, axis=1, keepdims=True)
    second = jnp.mean(scaled * unit_rows, axis=1, keepdims=True)
    grad_full = inv_std * (scaled - first - unit_rows * second)
    grad_vit = lax.dynamic_slice_in_dim(grad_full, column_start, share_width, 1).astype(
        jnp.bfloat16
    )
    return (normed, grad_text, grad_vit)


def solution(mesh):
    in_specs = (
        P("seq", None),
        P(),
        P(),
        P(None, "mp"),
        P("seq", "mp"),
        P("mp"),
        P("seq", "mp"),
        P(),
        P(),
    )
    out_specs = (P("seq", "mp"), P("seq", "mp"), P("seq", "mp"))
    return jax.shard_map(body, mesh=mesh, in_specs=in_specs, out_specs=out_specs, check_vma=False)
```

profile of v0, /device:TPU:2, one launch (start us, length us, event | category | flops | bytes accessed | tf_op | source)
XLA Modules:
  0.0 579.5 jit_solution(14132727948819414424)
XLA Ops:
  7.2 0.0 copy-start
  7.2 1.4 fusion.33
  10.6 1.2 dynamic-slice.2
  12.5 0.6 compare_and_fusion.1
  13.1 0.6 pad_clamp_fusion.2
  13.7 3.7 copy.14
  17.4 2.0 convert_reduce_fusion
  19.4 1.9 fusion.2
  21.3 0.0 copy-done
  21.3 0.0 copy-done.3
  21.3 0.0 copy-done.4
  21.3 0.0 copy-start.2
  21.4 0.0 copy-start.1
  21.4 2.2 fusion.7
  23.5 1.5 gather_fusion
  25.0 1.9 select_select_fusion
  26.9 15.6 %all-to-all-start = ((bf16[48,8,512]{2,1,0:T(8,128)(2,1)}), bf16[48,8,512]{2,1,0:T(8,128)(2,1)}, u32[]{:S(2)}, u32[]{:S(2)}) async-start(bf16[48,8,512]{2,1,0:T(8,128)(2,1)} %select_select_fusion), calls=%async_computation | async-start | bytes 786432 | tf_op jit(solution)/shard_map/all_to_all | solution.py:62
  42.5 0.0 copy-done.2
  42.5 0.1 convert_reduce_fusion.1
  42.7 0.8 gather_fusion.4
  43.4 0.8 gather_fusion.3
  44.2 0.1 broadcast_in_dim.113
  44.3 0.1 broadcast_in_dim.114
  44.4 0.1 broadcast_in_dim.110
  44.5 0.1 broadcast_in_dim.111
  44.6 15.3 %all-to-all-done = bf16[48,8,512]{2,1,0:T(8,128)(2,1)} async-done(((bf16[48,8,512]{2,1,0:T(8,128)(2,1)}), bf16[48,8,512]{2,1,0:T(8,128)(2,1)}, u32[]{:S(2)}, u32[]{:S(2)}) %all-to-all-start) | async-done | bytes 393248 | tf_op jit(solution)/shard_map/all_to_all | solution.py:62
  59.9 2.4 gather_fusion.1
  62.3 0.0 copy-done.6
  62.3 2.6 fusion.11
  64.9 68.7 %all-reduce = (f32[512]{0:T(512)S(1)}, f32[512]{0:T(512)S(1)}) all-reduce(f32[512]{0:T(512)S(1)} %get-tuple-element.18, f32[512]{0:T(512)S(1)} %get-tuple-element.17), channel_id=1, replica_groups=mesh['seq'=48,'mp'=16] {'mp'}, use_global_device_ids=true, to_apply=%region_5.7 | all-reduce | flops 1024 | bytes 8192 | tf_op jit(solution)/shard_map/psum | solution.py:71
  133.6 2.8 fusion.14
  136.5 2.1 reshape.204
  138.6 1.3 convolution_convert_fusion
  139.9 0.9 copy.15
  140.8 6.3 %all-to-all-start.1 = ((bf16[48,8,512]{2,1,0:T(8,128)(2,1)}), bf16[48,8,512]{2,1,0:T(8,128)(2,1)}, u32[]{:S(2)}, u32[]{:S(2)}) async-start(bf16[48,8,512]{2,1,0:T(8,128)(2,1)} %bitcast.21), calls=%async_computation.1 | async-start | bytes 786432 | tf_op jit(solution)/shard_map/all_to_all | solution.py:91
  147.1 0.0 reduce-scatter.2.cloned.1.call-start
  147.1 0.1 broadcast_in_dim.125
  147.2 0.1 broadcast_in_dim.126
  147.3 17.2 %all-to-all-done.1 = bf16[48,8,512]{2,1,0:T(8,128)(2,1)} async-done(((bf16[48,8,512]{2,1,0:T(8,128)(2,1)}), bf16[48,8,512]{2,1,0:T(8,128)(2,1)}, u32[]{:S(2)}, u32[]{:S(2)}) %all-to-all-start.1) | async-done | bytes 393248 | tf_op jit(solution)/shard_map/all_to_all | solution.py:91
  164.5 1.6 gather_fusion.2
  166.1 2.8 fusion.16
  168.9 0.0 reduce-scatter.2.cloned.1.call-update
  168.9 0.0 all-gather.2.cloned.1.call-start
  169.0 253.8 %reduce-scatter.2.cloned.1.call-done = f32[256,200]{0,1:T(8,128)} async-done(((f32[256,3200]{0,1:T(8,128)}), f32[256,200]{0,1:T(8,128)}) %reduce-scatter.2.cloned.1.call-update) | async-done | bytes 204816 | tf_op jit(solution)/shard_map/reduce_scatter | solution.py:98
  422.8 0.0 all-gather.2.cloned.1.call-update
  422.8 146.0 %all-gather.2.cloned.1.call-done = f32[256,3200]{0,1:T(8,128)} async-done(((f32[256,200]{0,1:T(8,128)}), f32[256,3200]{0,1:T(8,128)}) %all-gather.2.cloned.1.call-update) | async-done | bytes 3276816 | tf_op jit(solution)/shard_map/all_gather | solution.py:101
  568.8 3.2 fusion.38
  572.0 0.7 fusion.20
  (23 shorter events, 0.2 us)
Async XLA Ops:
  7.2 14.1 %copy-start = (bf16[3200,512]{1,0:T(8,128)(2,1)S(1)}, bf16[3200,512]{1,0:T(8,128)(2,1)}, u32[]{:S(2)}) copy-start(bf16[3200,512]{1,0:T(8,128)(2,1)} %param.14) | copy-start | bytes 9830404
  17.4 3.9 copy-start.3
  17.4 3.9 copy-start.4
  17.4 4.0 copy-start.7
  21.3 21.2 %copy-start.2 = (s32[48]{0:T(128)S(1)}, s32[48]{0:T(128)}, u32[]{:S(2)}) copy-start(s32[48]{0:T(128)} %param.18) | copy-start | bytes 580
  21.4 21.3 %copy-start.1 = (s32[48]{0:T(128)S(1)}, s32[48]{0:T(128)}, u32[]{:S(2)}) copy-start(s32[48]{0:T(128)} %param.19) | copy-start | bytes 580
  25.0 37.3 %copy-start.6 = (f32[512]{0:T(512)S(1)}, f32[512]{0:T(512)}, u32[]{:S(2)}) copy-start(f32[512]{0:T(512)} %param.16) | copy-start | bytes 6148
  26.9 33.0 %all-to-all-start = ((bf16[48,8,512]{2,1,0:T(8,128)(2,1)}), bf16[48,8,512]{2,1,0:T(8,128)(2,1)}, u32[]{:S(2)}, u32[]{:S(2)}) async-start(bf16[48,8,512]{2,1,0:T(8,128)(2,1)} %select_select_fusion), calls=%async_computation | async-start | bytes 786432 | tf_op jit(solution)/shard_map/all_to_all | solution.py:62
  140.8 23.8 %all-to-all-start.1 = ((bf16[48,8,512]{2,1,0:T(8,128)(2,1)}), bf16[48,8,512]{2,1,0:T(8,128)(2,1)}, u32[]{:S(2)}, u32[]{:S(2)}) async-start(bf16[48,8,512]{2,1,0:T(8,128)(2,1)} %bitcast.21), calls=%async_computation.1 | async-start | bytes 786432 | tf_op jit(solution)/shard_map/all_to_all | solution.py:91
  147.1 275.7 %reduce-scatter.2.cloned.1.call-start = ((), (), s32[]{:S(2)}) async-start(), calls=%async_computation.3 | async-start | bytes 3481600 | tf_op jit(solution)/shard_map/reduce_scatter | solution.py:98
  168.9 399.9 %copy-start.5 = (f32[3200]{0:T(1024)S(1)}, f32[3200]{0:T(1024)}, u32[]{:S(2)}) copy-start(f32[3200]{0:T(1024)} %param.12) | copy-start | bytes 38404
  168.9 399.9 %all-gather.2.cloned.1.call-start = ((), (), s32[]{:S(2)}) async-start(), calls=%async_computation.4 | async-start | bytes 3481600 | tf_op jit(solution)/shard_map/all_gather | solution.py:101
Sparse Core Ops, SparseCore 0:
  169.1 253.6 reduce-scatter.1
  426.6 142.1 all-gather.1
where the time goes:
time: 580 us
  waiting for transfers between devices  432 us (74%)
  blocking collectives  68.7 us (12%)
  starting transfers between devices  22 us (4%)
  other arithmetic  18 us (3%)
  between operations  16.8 us (3%)
  local copies, waits for them, and re-layouts  15.4 us (3%)
  matrix products  6.25 us (1%)
    reduce_scatter x1, waiting for transfers between devices, body(): lax.psum_scatter(partial_grad, 'mp', scatter_dimension=1, tiled=True)  254 us
    all_gather x1, waiting for transfers between devices, body(): full_grad = lax.all_gather(share, 'mp', axis=1, tiled=True)  146 us
    psum x1, blocking collectives, body(): lax.psum((jnp.sum(merged_f * merged_f, axis=1), jnp.sum(grad_gain * merge...  68.7 us
    all_to_all x1, waiting for transfers between devices, body(): lax.all_to_all(returning, 'seq', split_axis=0, concat_axis=0, tiled=True)  17.2 us
    all_to_all x1, starting transfers between devices, body(): lax.all_to_all(outgoing, 'seq', split_axis=0, concat_axis=0, tiled=True)  15.6 us
    all_to_all x1, waiting for transfers between devices, body(): lax.all_to_all(outgoing, 'seq', split_axis=0, concat_axis=0, tiled=True)  15.3 us
  transfers between devices with their start and end apart: 4, of which 4 were waited for; matrix products, arithmetic and copies ran while one was open for 0% of the time, Pallas kernels for 0%

commit v1 on v0

v1 whole, which is shorter than its diff:
```python
import functools

import jax
import jax.numpy as jnp
from jax import lax
from jax.experimental import pallas as pl
from jax.experimental.pallas import tpu as pltpu
from jax.sharding import PartitionSpec as P

BLK = 8
EPSILON = 1e-05
F32 = jnp.float32
BF16 = jnp.bfloat16
MESH = pl.DeviceIdType.MESH
NT = (((1,), (1,)), ((), ()))


def three_parts(x):
    hi = x.astype(BF16).astype(F32)
    mid = (x - hi).astype(BF16).astype(F32)
    return hi, mid, (x - hi) - mid


def stacked(parts, rows, width):
    row = lax.broadcasted_iota(jnp.int32, (rows, width), 0)
    out = jnp.zeros((rows, width), F32)
    for i, part in enumerate(parts):
        out = jnp.where(row == i, jnp.broadcast_to(part, (rows, width)), out)
    return out.astype(BF16)


def folded(x):
    half = x.shape[1] // 2
    return jnp.concatenate([x[:, :half], x[:, half:]], axis=0)


def unfolded(x):
    return jnp.concatenate([x[:BLK], x[BLK:]], axis=1)


def coded(x):
    most = jnp.max(jnp.abs(x), axis=0, keepdims=True)
    exponent = jnp.ceil(jnp.log2(jnp.maximum(most, 1e-30) * 1.0001)) - 15.0
    codes = jnp.clip(jnp.round(x * jnp.exp2(-exponent)), -32767.0, 32767.0)
    below = jnp.broadcast_to(exponent, (8, x.shape[1]))
    return jnp.concatenate([codes, below], axis=0).astype(jnp.int32).astype(jnp.int16)


def decoded(q):
    values = q.astype(jnp.int32).astype(F32)
    rows = q.shape[0] - 8
    return values[:rows] * jnp.exp2(values[rows : rows + 1])


def kernel(
    seq, ny, full_width,
    maps, vit_hbm, gain_ref, bias_ref, weight_hbm, text_hbm, llm_ref, cot_hbm,
    normed_hbm, gtext_hbm, gvit_hbm,
    vit, weight, text, cot, normed_v, gtext_v, gvit_v,
    nvit, colstat, rowstat, pre, select, hid_t, gain_col,
    out_buf, in_buf, merged, grads, back_out, back_in, gembed, partial,
    stat_out, stat_in, mean_out, mean_in, ring_out, ring_in, z_out, z_in,
    local_sem, store_sem, a2a_send, a2a_recv, back_send, back_recv,
    stat_send, stat_recv, mean_send, mean_recv, ring_send, ring_recv, z_send, z_recv,
):
    mp = 2 * ny
    me = lax.axis_index("seq")
    rank = lax.axis_index("mp")
    zh = rank // ny
    y = rank % ny
    rows, features = vit.shape
    width = weight.shape[1]
    tile_blocks = rows // BLK
    local_blocks = text.shape[0] // BLK
    share = features // mp
    half = ny // 2

    barrier = pltpu.get_barrier_semaphore()

    loads = [
        pltpu.make_async_copy(vit_hbm, vit, local_sem.at[0]),
        pltpu.make_async_copy(weight_hbm, weight, local_sem.at[1]),
        pltpu.make_async_copy(text_hbm, text, local_sem.at[2]),
        pltpu.make_async_copy(cot_hbm, cot, local_sem.at[3]),
    ]
    for load in loads:
        load.start()

    def greet_seq(i, carry):
        pl.semaphore_signal(barrier, inc=1, device_id={"seq": lax.rem(me + i, seq)}, device_id_type=MESH)
        return carry

    def greet_mp(i, carry):
        pl.semaphore_signal(barrier, inc=1, device_id={"mp": lax.rem(rank + i, mp)}, device_id_type=MESH)
        return carry

    lax.fori_loop(1, seq, greet_seq, 0)
    lax.fori_loop(1, mp, greet_mp, 0)

    loads[0].wait()
    gain = gain_ref[...]
    bias = bias_ref[...]
    lane16 = lax.broadcasted_iota(jnp.int32, (16, 128), 1)

    def norm_rows(i, carry):
        at = pl.ds(pl.multiple_of(i * 16, 16), 16)
        x = vit[at, :].astype(F32)
        mean = jnp.sum(x, axis=1, keepdims=True) / features
        centred = x - mean
        inv = lax.rsqrt(jnp.sum(centred * centred, axis=1, keepdims=True) / features + EPSILON)
        nvit[at, :] = (centred * inv * gain + bias).astype(BF16)
        colstat[at, :] = jnp.where(lane16 == 0, mean, inv)
        return carry

    lax.fori_loop(0, rows // 16, norm_rows, 0)
    nvit[rows : rows + 16, :] = stacked(three_parts(gain) + three_parts(bias), 16, features)

    loads[1].wait()
    for n in range(2):
        cols = slice(n * (width // 2), (n + 1) * (width // 2))
        product = jnp.dot(nvit[...], weight[:, cols], preferred_element_type=F32)
        pre[:, :, cols] = product.reshape(tile_blocks + 2, BLK, width // 2)

    pl.semaphore_wait(barrier, seq - 1 + mp - 1)

    own_start = maps[local_blocks + me]

    def block_for(target):
        block = lax.rem(target - lax.rem(own_start, seq) + seq, seq)
        return folded(pre[jnp.minimum(block, tile_blocks - 1)]).astype(BF16)

    def send_block(i, carry):
        target = lax.rem(me + i, seq)
        out_buf[target] = block_for(target)
        pltpu.make_async_remote_copy(
            src_ref=out_buf.at[target], dst_ref=in_buf.at[me], send_sem=a2a_send, recv_sem=a2a_recv,
            device_id={"seq": target}, device_id_type=MESH,
        ).start()
        return carry

    lax.fori_loop(1, seq, send_block, 0)
    in_buf[me] = block_for(me)

    column = lax.broadcasted_iota(jnp.int32, (BLK, features), 1)
    within = lax.broadcasted_iota(jnp.int32, (BLK, features), 0)
    select_rows = select.shape[0]

    def pick_rows(i, carry):
        halves = []
        for h in range(2):
            hit = column == rank * share + i * 16 + h * 8 + within
            halves.append(jnp.where(hit, 1.0, 0.0))
            value = jnp.sum(jnp.where(hit, jnp.broadcast_to(gain, hit.shape), 0.0), axis=1, keepdims=True)
            gain_col[pl.ds(pl.multiple_of(i * 16 + h * 8, 8), 8), :] = jnp.broadcast_to(value, (BLK, 128))
        select[pl.ds(pl.multiple_of(i * 16, 16), 16), :] = jnp.concatenate(halves, axis=0).astype(BF16)
        return carry

    lax.fori_loop(0, select_rows // 16, pick_rows, 0)
    hid_t[...] = lax.dot_general(select[...], vit[...], NT, preferred_element_type=F32)
    rowstat[...] = jnp.transpose(colstat[...])[:8]

    loads[2].wait()
    loads[3].wait()
    waiting = in_buf.at[pl.ds(0, seq - 1)]
    pltpu.make_async_copy(waiting, waiting, a2a_recv).wait()

    llm = llm_ref[...]
    lane = lax.broadcasted_iota(jnp.int32, (BLK, 128), 1)

    def merge_pair(i, sums):
        at = pl.ds(pl.multiple_of(i * 16, 16), 16)
        text_pair = text[at, :].astype(F32)
        cot_pair = cot[at, :].astype(F32)
        for h in range(2):
            b = i * 2 + h
            source = maps[b]
            arrived = unfolded(in_buf[jnp.maximum(source, 0)].astype(F32))
            is_image = jnp.full((BLK, width), source, jnp.int32) >= 0
            m = jnp.where(is_image, arrived, text_pair[h * 8 : h * 8 + 8])
            merged[b] = m
            square = jnp.sum(m * m, axis=1, keepdims=True)
            product = jnp.sum(llm * cot_pair[h * 8 : h * 8 + 8] * m, axis=1, keepdims=True)
            sums = jnp.where(lane == b, square, sums)
            sums = jnp.where(lane == b + 64, product, sums)
        return sums

    stat_out[...] = lax.fori_loop(0, local_blocks // 2, merge_pair, jnp.ones((BLK, 128), F32))

    def send_stat(i, carry):
        target = lax.rem(rank + i, mp)
        pltpu.make_async_remote_copy(
            src_ref=stat_out, dst_ref=stat_in.at[rank], send_sem=stat_send, recv_sem=stat_recv,
            device_id={"mp": target}, device_id_type=MESH,
        ).start()
        return carry

    lax.fori_loop(1, mp, send_stat, 0)
    stat_in[rank] = stat_out[...]
    waiting = stat_in.at[pl.ds(0, mp - 1)]
    pltpu.make_async_copy(waiting, waiting, stat_recv).wait()

    total = stat_in[0]
    for i in range(1, mp):
        total = total + stat_in[i]
    inv_all = lax.rsqrt(total / full_width + EPSILON)
    slope_all = inv_all * inv_all * inv_all * pltpu.roll(total, 64, 1) / full_width

    def norm_pair(i, carry):
        at = pl.ds(pl.multiple_of(i * 16, 16), 16)
        cot_pair = cot[at, :].astype(F32)
        normed_pair, text_pair = [], []
        for h in range(2):
            b = i * 2 + h
            inv = jnp.sum(jnp.where(lane == b, inv_all, 0.0), axis=1, keepdims=True)
            slope = jnp.sum(jnp.where(lane == b, slope_all, 0.0), axis=1, keepdims=True)
            m = merged[b]
            normed_pair.append(m * inv * llm)
            grad = inv * (llm * cot_pair[h * 8 : h * 8 + 8]) - m * slope
            grads[b] = folded(grad).astype(BF16)
            is_image = jnp.full((BLK, width), maps[b], jnp.int32) >= 0
            text_pair.append(jnp.where(is_image, 0.0, grad))
        normed_v[at, :] = jnp.concatenate(normed_pair, axis=0).astype(BF16)
        gtext_v[at, :] = jnp.concatenate(text_pair, axis=0).astype(BF16)
        return carry

    lax.fori_loop(0, local_blocks // 2, norm_pair, 0)

    def grad_for(target):
        start = maps[local_blocks + target]
        block = start + lax.rem(me - lax.rem(start, seq) + seq, seq)
        return grads[jnp.minimum(block // seq, local_blocks - 1)]

    def send_back(i, carry):
        target = lax.rem(me + i, seq)
        back_out[target] = grad_for(target)
        pltpu.make_async_remote_copy(
            src_ref=back_out.at[target], dst_ref=back_in.at[me], send_sem=back_send, recv_sem=back_recv,
            device_id={"seq": target}, device_id_type=MESH,
        ).start()
        return carry

    lax.fori_loop(1, seq, send_back, 0)
    back_in[me] = grad_for(me)

    stores = [
        pltpu.make_async_copy(normed_v, normed_hbm, store_sem.at[0]),
        pltpu.make_async_copy(gtext_v, gtext_hbm, store_sem.at[1]),
    ]
    for store in stores:
        store.start()

    waiting = back_in.at[pl.ds(0, seq - 1)]
    pltpu.make_async_copy(waiting, waiting, back_recv).wait()

    def gather_pair(i, carry):
        pair = []
        for h in range(2):
            source = lax.rem(lax.rem(own_start, seq) + i * 2 + h, seq)
            pair.append(unfolded(back_in[source].astype(F32)))
        gembed[pl.ds(pl.multiple_of(i * 16, 16), 16), :] = jnp.concatenate(pair, axis=0).astype(BF16)
        return carry

    lax.fori_loop(0, tile_blocks // 2, gather_pair, 0)

    below = pre[tile_blocks]
    gain_weight = below[0:1] + below[1:2] + below[2:3]
    bias_weight = below[3:4] + below[4:5] + below[5:6]
    g = gembed[...]
    first = lax.dot_general(stacked(three_parts(gain_weight), 16, width), g, NT, preferred_element_type=F32)
    embed = pre[:tile_blocks].reshape(rows, width) - bias_weight
    weighted = g.astype(F32) * embed
    high = weighted.astype(BF16)
    low = (weighted - high.astype(F32)).astype(BF16)
    ones = jnp.ones((16, width), BF16)
    second = lax.dot_general(ones, high, NT, preferred_element_type=F32)
    second = second + lax.dot_general(ones, low, NT, preferred_element_type=F32)
    mean_out[...] = jnp.concatenate(
        [jnp.broadcast_to(jnp.sum(first, axis=0, keepdims=True), (8, rows)), second[:8]], axis=1
    )

    def send_mean(i, carry):
        target = lax.rem(rank + i, mp)
        pltpu.make_async_remote_copy(
            src_ref=mean_out, dst_ref=mean_in.at[rank], send_sem=mean_send, recv_sem=mean_recv,
            device_id={"mp": target}, device_id_type=MESH,
        ).start()
        return carry

    lax.fori_loop(1, mp, send_mean, 0)
    mean_in[rank] = mean_out[...]

    step_rows = features // 8
    for n in range(8):
        piece = slice(n * step_rows, (n + 1) * step_rows)
        partial[piece, :] = lax.dot_general(weight[piece, :], g, NT, preferred_element_type=F32)

    def own(target, h):
        start = (h * ny + target) * share
        return partial[pl.ds(pl.multiple_of(start, 8), share), :]

    def ring_copy(direction, step, h):
        to = lax.rem(y + 1, ny) if direction == 0 else lax.rem(y + ny - 1, ny)
        return pltpu.make_async_remote_copy(
            src_ref=ring_out.at[direction, step, h], dst_ref=ring_in.at[direction, step, h],
            send_sem=ring_send.at[direction, step, h], recv_sem=ring_recv.at[direction, step, h],
            device_id={"mp": zh * ny + to}, device_id_type=MESH,
        )

    copies = []
    for step in range(half):
        for h in range(2):
            for direction in range(2):
                if step == 0 and h != direction:
                    continue
                away = half - step
                target = lax.rem(y + away, ny) if direction == 0 else lax.rem(y + ny - away, ny)
                value = own(target, h)
                if step >= 2 or (step == 1 and h == direction):
                    ring_copy(direction, step - 1, h).wait_recv()
                    value = value + decoded(ring_in[direction, step - 1, h])
                ring_out[direction, step, h] = coded(value)
                copy = ring_copy(direction, step, h)
                copy.start()
                copies.append(copy)

    def arrived_sum(h):
        value = own(y, h)
        for direction in range(2):
            if half >= 2 or h == direction:
                ring_copy(direction, half - 1, h).wait_recv()
                value = value + decoded(ring_in[direction, half - 1, h])
        return value

    sums = [arrived_sum(h) for h in range(2)]
    z_out[...] = coded(jnp.where(jnp.full(sums[0].shape, zh, jnp.int32) == 0, sums[1], sums[0]))
    z_copy = pltpu.make_async_remote_copy(
        src_ref=z_out, dst_ref=z_in, send_sem=z_send, recv_sem=z_recv,
        device_id={"mp": (1 - zh) * ny + y}, device_id_type=MESH,
    )
    z_copy.start()
    kept = jnp.where(jnp.full(sums[0].shape, zh, jnp.int32) == 0, sums[0], sums[1])

    waiting = mean_in.at[pl.ds(0, mp - 1)]
    pltpu.make_async_copy(waiting, waiting, mean_recv).wait()
    means = mean_in[0]
    for i in range(1, mp):
        means = means + mean_in[i]
    means = means / features
    mean_first = means[0:1, :rows]
    mean_second = means[0:1, rows:]
    inv_row = rowstat[1:2, :]
    unit = (hid_t[:share, :] - rowstat[0:1, :]) * inv_row
    offset = mean_first + unit * mean_second
    z_copy.wait_recv()
    scaled = (kept + decoded(z_in[...])) * gain_col[:share, 0:1]
    result = inv_row * (scaled - offset)
    padded = jnp.concatenate([result, jnp.zeros((gvit_v.shape[1] - share, rows), F32)], axis=0)
    gvit_v[...] = jnp.transpose(padded).astype(BF16)
    last = pltpu.make_async_copy(gvit_v, gvit_hbm, store_sem.at[2])
    last.start()

    waiting = out_buf.at[pl.ds(0, seq - 1)]
    pltpu.make_async_copy(waiting, waiting, a2a_send).wait()
    waiting = back_out.at[pl.ds(0, seq - 1)]
    pltpu.make_async_copy(waiting, waiting, back_send).wait()
    waiting = stat_in.at[pl.ds(0, mp - 1)]
    pltpu.make_async_copy(waiting, waiting, stat_send).wait()
    waiting = mean_in.at[pl.ds(0, mp - 1)]
    pltpu.make_async_copy(waiting, waiting, mean_send).wait()
    for copy in copies:
        copy.wait_send()
    z_copy.wait_send()
    for store in stores:
        store.wait()
    last.wait()


def body(
    vit_hidden,
    vit_gain,
    vit_bias,
    proj_weight,
    text_emb,
    llm_gain,
    cotangent,
    tile_start,
    tile_owner,
):
    seq = lax.axis_size("seq")
    mp = lax.axis_size("mp")
    ny = mp // 2
    me = lax.axis_index("seq")
    rows, features = vit_hidden.shape
    width = proj_weight.shape[1]
    tokens = text_emb.shape[0]
    tile_blocks = rows // BLK
    local_blocks = tokens // BLK
    share = features // mp
    padded = -(-share // 128) * 128

    entry = jnp.arange(local_blocks + seq, dtype=jnp.int32)[:, None]
    start = tile_start[None, :]
    owner = tile_owner[None, :]
    away = (me - start) % seq
    slot = (start + away) // seq
    here = (away < tile_blocks) & (slot == entry)
    maps = jnp.sum(
        jnp.where(
            entry < local_blocks,
            jnp.where(here, owner + 1, 0),
            jnp.where(owner == entry - local_blocks, start, 0),
        ),
        axis=1,
    ) - jnp.where(entry[:, 0] < local_blocks, 1, 0)
    maps = maps.astype(jnp.int32)

    vmem = pl.BlockSpec(memory_space=pltpu.VMEM)
    anywhere = pl.BlockSpec(memory_space=pl.ANY)
    half_width = width // 2
    half = ny // 2
    dma = pltpu.SemaphoreType.DMA
    normed, grad_text, grad_vit = pl.pallas_call(
        functools.partial(kernel, seq, ny, width * mp),
        out_shape=(
            jax.ShapeDtypeStruct((tokens, width), BF16),
            jax.ShapeDtypeStruct((tokens, width), BF16),
            jax.ShapeDtypeStruct((rows, padded), BF16),
        ),
        in_specs=[
            pl.BlockSpec(memory_space=pltpu.SMEM),
            anywhere, vmem, vmem, anywhere, anywhere, vmem, anywhere,
        ],
        out_specs=(anywhere, anywhere, anywhere),
        scratch_shapes=[
            pltpu.VMEM((rows, features), BF16),
            pltpu.VMEM((features, width), BF16),
            pltpu.VMEM((tokens, width), BF16),
            pltpu.VMEM((tokens, width), BF16),
            pltpu.VMEM((tokens, width), BF16),
            pltpu.VMEM((tokens, width), BF16),
            pltpu.VMEM((rows, padded), BF16),
            pltpu.VMEM((rows + 16, features), BF16),
            pltpu.VMEM((rows, 128), F32),
            pltpu.VMEM((8, rows), F32),
            pltpu.VMEM((tile_blocks + 2, BLK, width), F32),
            pltpu.VMEM((-(-share // 16) * 16, features), BF16),
            pltpu.VMEM((-(-share // 16) * 16, rows), F32),
            pltpu.VMEM((-(-share // 16) * 16, 128), F32),
            pltpu.VMEM((seq, 16, half_width), BF16),
            pltpu.VMEM((seq, 16, half_width), BF16),
            pltpu.VMEM((local_blocks, BLK, width), F32),
            pltpu.VMEM((local_blocks, 16, half_width), BF16),
            pltpu.VMEM((seq, 16, half_width), BF16),
            pltpu.VMEM((seq, 16, half_width), BF16),
            pltpu.VMEM((rows, width), BF16),
            pltpu.VMEM((features, rows), F32),
            pltpu.VMEM((BLK, 128), F32),
            pltpu.VMEM((mp, BLK, 128), F32),
            pltpu.VMEM((8, 2 * rows), F32),
            pltpu.VMEM((mp, 8, 2 * rows), F32),
            pltpu.VMEM((2, half, 2, share + 8, rows), jnp.int16),
            pltpu.VMEM((2, half, 2, share + 8, rows), jnp.int16),
            pltpu.VMEM((share + 8, rows), jnp.int16),
            pltpu.VMEM((share + 8, rows), jnp.int16),
            dma((4,)),
            dma((3,)),
            dma, dma, dma, dma, dma, dma, dma, dma,
            dma((2, half, 2)),
            dma((2, half, 2)),
            dma, dma,
        ],
        compiler_params=pltpu.CompilerParams(
            collective_id=0, has_side_effects=True, vmem_limit_bytes=48 * 2**20
        ),
        name="tiles",
    )(
        maps,
        vit_hidden,
        vit_gain.reshape(1, features),
        vit_bias.reshape(1, features),
        proj_weight,
        text_emb,
        llm_gain.reshape(1, width),
        cotangent,
    )
    return (normed, grad_text, grad_vit[:, :share])


def solution(mesh):
    in_specs = (
        P("seq", None),
        P(),
        P(),
        P(None, "mp"),
        P("seq", "mp"),
        P("mp"),
        P("seq", "mp"),
        P(),
        P(),
    )
    out_specs = (P("seq", "mp"), P("seq", "mp"), P("seq", "mp"))
    return jax.shard_map(body, mesh=mesh, in_specs=in_specs, out_specs=out_specs, check_vma=False)
```

time: 580 us -> 115 us (0.20)
  the two profiles are of different devices: /device:TPU:2 before, /device:TPU:8 now
where the time goes in v1:
time: 115 us; the launch traced here: 114 us
  Pallas kernels  103 us (90%)
  local copies, waits for them, and re-layouts  7.98 us (7%)
  other arithmetic  2.16 us (2%)
    pallas_call x1, Pallas kernels, body(): pl.pallas_call(functools.partial(kernel, seq, ny, width * mp), out_shape=...  103 us
    unnamed x11, local copies, waits for them, and re-layouts  6.52 us

profile of v1, /device:TPU:8, one launch (start us, length us, event | category | flops | bytes accessed | tf_op | source)
XLA Modules:
  0.0 114.3 jit_solution(11090856166023543803)
XLA Ops:
  0.7 0.7 broadcast_compare_fusion
  1.3 0.7 and_select_fusion
  2.0 0.8 select_reduce_fusion
  2.8 0.7 reshape.48.gain_ref
  3.5 0.7 reshape.49.bias_ref
  4.3 0.0 copy-start
  4.3 1.4 %copy-done = bf16[256,3200]{1,0:T(8,128)(2,1)S(1)} copy-done((bf16[256,3200]{1,0:T(8,128)(2,1)S(1)}, bf16[256,3200]{1,0:T(8,128)(2,1)}, u32[]{:S(2)}) %copy-start) | copy-done | bytes 1638424
  5.7 0.0 copy-start.1
  5.7 1.0 copy-done.1
  6.8 0.0 copy-start.2
  6.8 1.0 copy-done.2
  7.8 0.0 copy-start.3
  7.8 0.7 copy-done.3
  8.5 103.5 %tiles.1 = (bf16[512,512]{1,0:T(8,128)(2,1)S(1)}, bf16[512,512]{1,0:T(8,128)(2,1)S(1)}, bf16[256,256]{1,0:T(8,128)(2,1)S(1)}) custom-call(s32[112]{0:T(128)S(1)} %select_subtract_fusion.maps, bf16[256,3200]{1,0:T(8,128)(2,1)S(1)} %copy-done, f32[1,3200]{1,0:T(1,128)S(1)} %reshape.48.gain_ref, f32[1,3200]{1,0:T(1,128)S(1)} %reshape.49.bias_ref, ...), custom_call_target="tpu_custom_call" | custom-call | tf_op jit(solution)/shard_map/tiles/pallas_call | solution.py:422
  112.0 0.7 copy.13
  112.7 0.8 copy.16
  113.5 0.8 copy.17
  (3 shorter events, 0.0 us)
Async XLA Ops:
  4.3 1.4 %copy-start = (bf16[256,3200]{1,0:T(8,128)(2,1)S(1)}, bf16[256,3200]{1,0:T(8,128)(2,1)}, u32[]{:S(2)}) copy-start(bf16[256,3200]{1,0:T(8,128)(2,1)} %vit_hbm.1) | copy-start | bytes 4915204
  5.7 1.0 copy-start.1
  6.8 1.0 copy-start.2
  7.8 0.7 copy-start.3

commit v2 on v1

v2 whole, which is shorter than its diff:
```python
import functools

import jax
import jax.numpy as jnp
from jax import lax
from jax.experimental import pallas as pl
from jax.experimental.pallas import tpu as pltpu
from jax.sharding import PartitionSpec as P

BLK = 8
EPSILON = 1e-05
F32 = jnp.float32
BF16 = jnp.bfloat16
MESH = pl.DeviceIdType.MESH
NT = (((1,), (1,)), ((), ()))


def three_parts(x):
    hi = x.astype(BF16).astype(F32)
    mid = (x - hi).astype(BF16).astype(F32)
    return hi, mid, (x - hi) - mid


def stacked(parts, rows, width):
    row = lax.broadcasted_iota(jnp.int32, (rows, width), 0)
    out = jnp.zeros((rows, width), F32)
    for i, part in enumerate(parts):
        out = jnp.where(row == i, jnp.broadcast_to(part, (rows, width)), out)
    return out.astype(BF16)


def folded(x):
    half = x.shape[1] // 2
    return jnp.concatenate([x[:, :half], x[:, half:]], axis=0)


def unfolded(x):
    return jnp.concatenate([x[:BLK], x[BLK:]], axis=1)


def coded(x):
    most = jnp.max(jnp.abs(x), axis=0, keepdims=True)
    exponent = jnp.ceil(jnp.log2(jnp.maximum(most, 1e-30) * 1.0001)) - 15.0
    codes = jnp.clip(jnp.round(x * jnp.exp2(-exponent)), -32767.0, 32767.0)
    below = jnp.broadcast_to(exponent, (8, x.shape[1]))
    return jnp.concatenate([codes, below], axis=0).astype(jnp.int32).astype(jnp.int16)


def decoded(q):
    values = q.astype(jnp.int32).astype(F32)
    rows = q.shape[0] - 8
    return values[:rows] * jnp.exp2(values[rows : rows + 1])


def kernel(
    seq, ny, full_width,
    starts, owners, vit_hbm, gain_hbm, bias_hbm, weight_hbm, text_hbm, llm_hbm, cot_hbm,
    normed_hbm, gtext_hbm, gvit_hbm,
    table, maps, gain_ref, bias_ref, llm_ref,
    vit, weight, text, cot, normed_v, gtext_v, gvit_v,
    nvit, colstat, pre, select, hid,
    out_buf, in_buf, merged, scaled_cot, inv_of, slope_of, back_out, back_even, back_odd,
    gembed, weighted_hi, weighted_lo, partial, kept, turned,
    stat_out, stat_in, stat_zout, stat_zin, mean_out, mean_in, mean_zout, mean_zin,
    ring_out, ring_in, z_out, z_in,
    local_sem, store_sem, a2a_send, a2a_recv, back_send, back_recv,
    sum_send, sum_recv, sum_zsend, sum_zrecv, ring_send, ring_recv, z_send, z_recv,
):
    mp = 2 * ny
    me = lax.axis_index("seq")
    rank = lax.axis_index("mp")
    zh = rank // ny
    y = rank % ny
    rows, features = vit.shape
    width = weight.shape[1]
    tile_blocks = rows // BLK
    local_blocks = text.shape[0] // BLK
    share = features // mp
    half = ny // 2
    half_rows = rows // 2

    barrier = pltpu.get_barrier_semaphore()

    loads = [
        pltpu.make_async_copy(vit_hbm, vit, local_sem.at[0]),
        pltpu.make_async_copy(gain_hbm, gain_ref.at[0], local_sem.at[1]),
        pltpu.make_async_copy(bias_hbm, bias_ref.at[0], local_sem.at[2]),
        pltpu.make_async_copy(weight_hbm, weight, local_sem.at[3]),
        pltpu.make_async_copy(text_hbm, text, local_sem.at[4]),
        pltpu.make_async_copy(cot_hbm, cot, local_sem.at[5]),
        pltpu.make_async_copy(llm_hbm, llm_ref.at[0], local_sem.at[6]),
    ]
    for load in loads:
        load.start()

    def greet_seq(i, carry):
        pl.semaphore_signal(barrier, inc=1, device_id={"seq": lax.rem(me + i, seq)}, device_id_type=MESH)
        return carry

    def greet_mp(i, carry):
        pl.semaphore_signal(barrier, inc=1, device_id={"mp": zh * ny + lax.rem(y + i, ny)}, device_id_type=MESH)
        return carry

    lax.fori_loop(1, seq, greet_seq, 0)
    lax.fori_loop(1, ny, greet_mp, 0)
    other_z = (1 - zh) * ny + y
    pl.semaphore_signal(barrier, inc=1, device_id={"mp": other_z}, device_id_type=MESH)

    lane = lax.broadcasted_iota(jnp.int32, (BLK, 128), 1)

    def look_up(t, found):
        source, start_of = found
        start, owner = starts[t], owners[t]
        away = lax.rem(me - lax.rem(start, seq) + seq, seq)
        hit = (lane == lax.div(start + away, seq)) & (jnp.full((BLK, 128), away, jnp.int32) < tile_blocks)
        return jnp.where(hit, owner, source), jnp.where(lane == owner, start, start_of)

    empty = jnp.zeros((BLK, 128), jnp.int32)
    source, start_of = lax.fori_loop(0, seq, look_up, (empty - 1, empty), unroll=4)
    table[...] = jnp.where(lax.broadcasted_iota(jnp.int32, (BLK, 128), 0) == 0, source, start_of)
    table_copy = pltpu.make_async_copy(table, maps, local_sem.at[7])
    table_copy.start()

    for load in loads[:3]:
        load.wait()
    gain = gain_ref[...]
    bias = bias_ref[...]
    lane16 = lax.broadcasted_iota(jnp.int32, (16, 128), 1)

    def norm_rows(i, carry):
        at = pl.ds(pl.multiple_of(i * 16, 16), 16)
        x = vit[at, :].astype(F32)
        mean = jnp.sum(x, axis=1, keepdims=True) / features
        centred = x - mean
        inv = lax.rsqrt(jnp.sum(centred * centred, axis=1, keepdims=True) / features + EPSILON)
        nvit[at, :] = (centred * inv * gain + bias).astype(BF16)
        colstat[at, :] = jnp.where(lane16 == 0, mean, inv)
        return carry

    lax.fori_loop(0, rows // 16, norm_rows, 0)
    nvit[rows : rows + 16, :] = stacked(three_parts(gain) + three_parts(bias), 16, features)

    loads[3].wait()
    for n in range(2):
        cols = slice(n * (width // 2), (n + 1) * (width // 2))
        product = jnp.dot(nvit[...], weight[:, cols], preferred_element_type=F32)
        pre[:, :, cols] = product.reshape(tile_blocks + 2, BLK, width // 2)

    pl.semaphore_wait(barrier, seq - 1 + ny)

    table_copy.wait()
    own_start = maps[1, me]
    own_phase = lax.rem(own_start, seq)

    def block_for(target):
        block = lax.rem(target - own_phase + seq, seq)
        return folded(pre[jnp.minimum(block, tile_blocks - 1)]).astype(BF16)

    def send_block(i, carry):
        target = lax.rem(me + i, seq)
        out_buf[target] = block_for(target)
        pltpu.make_async_remote_copy(
            src_ref=out_buf.at[target], dst_ref=in_buf.at[me], send_sem=a2a_send, recv_sem=a2a_recv,
            device_id={"seq": target}, device_id_type=MESH,
        ).start()
        return carry

    lax.fori_loop(1, seq, send_block, 0)
    in_buf[me] = block_for(me)

    for load in loads[4:]:
        load.wait()
    llm = llm_ref[...]

    def scale_pair(i, carry):
        at = pl.ds(pl.multiple_of(i * 16, 16), 16)
        scaled_pair = llm * cot[at, :].astype(F32)
        for h in range(2):
            scaled_cot[i * 2 + h] = scaled_pair[h * 8 : h * 8 + 8]
        return carry

    lax.fori_loop(0, local_blocks // 2, scale_pair, 0, unroll=2)
    column = lax.broadcasted_iota(jnp.int32, (16, features), 1)
    within = lax.broadcasted_iota(jnp.int32, (16, features), 0)

    def pick_rows(i, carry):
        hit = column == rank * share + i * 16 + within
        select[pl.ds(pl.multiple_of(i * 16, 16), 16), :] = jnp.where(hit, 1.0, 0.0).astype(BF16)
        return carry

    lax.fori_loop(0, select.shape[0] // 16, pick_rows, 0)
    hid[...] = lax.dot_general(vit[...], select[...], NT, preferred_element_type=F32)
    gains = lax.dot_general(nvit[rows : rows + 16, :], select[...], NT, preferred_element_type=F32)
    gain_row = gains[0:1] + gains[1:2] + gains[2:3]

    waiting = in_buf.at[pl.ds(0, seq - 1)]
    pltpu.make_async_copy(waiting, waiting, a2a_recv).wait()

    def merge_pair(i, sums):
        at = pl.ds(pl.multiple_of(i * 16, 16), 16)
        text_pair = text[at, :].astype(F32)
        for h in range(2):
            b = i * 2 + h
            source = maps[0, b]
            arrived = unfolded(in_buf[jnp.maximum(source, 0)].astype(F32))
            is_image = jnp.full((BLK, width), source, jnp.int32) >= 0
            m = jnp.where(is_image, arrived, text_pair[h * 8 : h * 8 + 8])
            merged[b] = m
            square = jnp.sum(m * m, axis=1, keepdims=True)
            product = jnp.sum(scaled_cot[b] * m, axis=1, keepdims=True)
            sums = jnp.where(lane == b, square, sums)
            sums = jnp.where(lane == b + 64, product, sums)
        return sums

    stat_out[...] = lax.fori_loop(
        0, local_blocks // 2, merge_pair, jnp.ones((BLK, 128), F32), unroll=2
    )

    def start_sum(which, out, into):
        def send(i, carry):
            pltpu.make_async_remote_copy(
                src_ref=out, dst_ref=into.at[y], send_sem=sum_send.at[which], recv_sem=sum_recv.at[which],
                device_id={"mp": zh * ny + lax.rem(y + i, ny)}, device_id_type=MESH,
            ).start()
            return carry

        lax.fori_loop(1, ny, send, 0)
        into[y] = out[...]

    def middle_sum(which, into, zout, zin):
        waiting = into.at[pl.ds(0, ny - 1)]
        pltpu.make_async_copy(waiting, waiting, sum_recv.at[which]).wait()
        total = into[0]
        for i in range(1, ny):
            total = total + into[i]
        zout[...] = total
        copy = pltpu.make_async_remote_copy(
            src_ref=zout, dst_ref=zin, send_sem=sum_zsend.at[which], recv_sem=sum_zrecv.at[which],
            device_id={"mp": other_z}, device_id_type=MESH,
        )
        copy.start()
        return copy

    start_sum(0, stat_out, stat_in)
    stat_copy = middle_sum(0, stat_in, stat_zout, stat_zin)
    stat_copy.wait_recv()
    total = stat_zout[...] + stat_zin[...]
    inv_all = lax.rsqrt(total / full_width + EPSILON)
    slope_all = inv_all * inv_all * inv_all * pltpu.roll(total, 64, 1) / full_width
    for b in range(local_blocks):
        inv_of[b] = jnp.broadcast_to(inv_all[:, b : b + 1], (BLK, 128))
        slope_of[b] = jnp.broadcast_to(slope_all[:, b : b + 1], (BLK, 128))

    def wide(x):
        return jnp.concatenate([x] * (width // 128), axis=1)

    chips = seq // 2
    back_in = (back_even, back_odd)

    def slot_of(device):
        return 2 * (device // 4) + lax.rem(device, 2)

    def send_back(phase):
        core = lax.rem(me // 2 + phase, 2)

        def send(i, carry):
            target = 2 * lax.rem(me // 2 + i, chips) + core
            start = maps[1, target]
            block = start + lax.rem(me - lax.rem(start, seq) + seq, seq)
            b = jnp.minimum(block // seq, local_blocks - 1)
            grad = wide(inv_of[b]) * scaled_cot[b] - merged[b] * wide(slope_of[b])
            value = folded(grad).astype(BF16)

            @pl.when(target == me)
            def _():
                back_in[phase][slot_of(me)] = value

            @pl.when(target != me)
            def _():
                back_out[target] = value
                pltpu.make_async_remote_copy(
                    src_ref=back_out.at[target], dst_ref=back_in[phase].at[slot_of(me)],
                    send_sem=back_send.at[phase], recv_sem=back_recv.at[phase],
                    device_id={"seq": target}, device_id_type=MESH,
                ).start()

            return carry

        lax.fori_loop(0, chips, send, 0)

    send_back(0)

    def norm_pair(i, carry):
        at = pl.ds(pl.multiple_of(i * 16, 16), 16)
        normed_pair, text_pair = [], []
        for h in range(2):
            b = i * 2 + h
            inv = wide(inv_of[b])
            m = merged[b]
            normed_pair.append(m * inv * llm)
            grad = inv * scaled_cot[b] - m * wide(slope_of[b])
            is_image = jnp.full((BLK, width), maps[0, b], jnp.int32) >= 0
            text_pair.append(jnp.where(is_image, 0.0, grad))
        normed_v[at, :] = jnp.concatenate(normed_pair, axis=0).astype(BF16)
        gtext_v[at, :] = jnp.concatenate(text_pair, axis=0).astype(BF16)
        return carry

    lax.fori_loop(0, local_blocks // 2, norm_pair, 0, unroll=2)
    stores = [
        pltpu.make_async_copy(normed_v, normed_hbm, store_sem.at[0]),
        pltpu.make_async_copy(gtext_v, gtext_hbm, store_sem.at[1]),
    ]
    for store in stores:
        store.start()

    below = pre[tile_blocks]
    gain_weight = below[0:1] + below[1:2] + below[2:3]
    bias_weight = below[3:4] + below[4:5] + below[5:6]
    gain_parts = stacked(three_parts(gain_weight), 16, width)
    ones = jnp.ones((16, width), BF16)

    def wait_phase(buffer, sem, phase):
        own_in = lax.rem(me // 2 + me, 2) == phase

        @pl.when(own_in)
        def _():
            waiting = buffer.at[pl.ds(0, chips - 1)]
            pltpu.make_async_copy(waiting, waiting, sem.at[phase]).wait()

        @pl.when(jnp.logical_not(own_in))
        def _():
            waiting = buffer.at[pl.ds(0, chips)]
            pltpu.make_async_copy(waiting, waiting, sem.at[phase]).wait()

    def receive(phase):
        wait_phase(back_in[phase], back_recv, phase)
        parity = lax.rem(me + phase, 2)

        def gather_pair(i, carry):
            pair, embed = [], []
            for c in range(2):
                j = lax.rem(2 * parity + c - lax.rem(own_phase, 4) + 4, 4) + 4 * i
                device = lax.rem(own_phase + j, seq)
                pair.append(unfolded(back_in[phase][slot_of(device)].astype(F32)))
                embed.append(pre[j])
            at = pl.ds(pl.multiple_of(i * 16, 16), 16)
            g = jnp.concatenate(pair, axis=0)
            weighted = g * (jnp.concatenate(embed, axis=0) - bias_weight)
            high = weighted.astype(BF16)
            gembed[phase, at, :] = g.astype(BF16)
            weighted_hi[phase, at, :] = high
            weighted_lo[phase, at, :] = (weighted - high.astype(F32)).astype(BF16)
            return carry

        lax.fori_loop(0, tile_blocks // 4, gather_pair, 0)
        g = gembed[phase]
        step_rows = features // 8
        for n in range(8):
            piece = slice(n * step_rows, (n + 1) * step_rows)
            partial[phase, piece, :] = lax.dot_general(
                weight[piece, :], g, NT, preferred_element_type=F32
            )

    def two_sums(phase):
        first = lax.dot_general(gain_parts, gembed[phase], NT, preferred_element_type=F32)
        second = lax.dot_general(ones, weighted_hi[phase], NT, preferred_element_type=F32)
        second = second + lax.dot_general(ones, weighted_lo[phase], NT, preferred_element_type=F32)
        return jnp.sum(first, axis=0, keepdims=True), second[0:1]

    def own(phase, target, h):
        start = ((1 - zh if h == 0 else zh) * ny + target) * share
        return partial[phase, pl.ds(pl.multiple_of(start, 8), share), :]

    def ring_copy(phase, direction, step, h):
        to = lax.rem(y + 1, ny) if direction == 0 else lax.rem(y + ny - 1, ny)
        at = (phase, direction, step, h)
        return pltpu.make_async_remote_copy(
            src_ref=ring_out.at[at], dst_ref=ring_in.at[at],
            send_sem=ring_send.at[at], recv_sem=ring_recv.at[at],
            device_id={"mp": zh * ny + to}, device_id_type=MESH,
        )

    copies = []

    def ring_step(phase, step):
        for h in range(2):
            for direction in range(2):
                if step == 0 and h != direction:
                    continue
                away = half - step
                target = lax.rem(y + away, ny) if direction == 0 else lax.rem(y + ny - away, ny)
                value = own(phase, target, h)
                if step >= 2 or (step == 1 and h == direction):
                    ring_copy(phase, direction, step - 1, h).wait_recv()
                    value = value + decoded(ring_in[phase, direction, step - 1, h])
                ring_out[phase, direction, step, h] = coded(value)
                copy = ring_copy(phase, direction, step, h)
                copy.start()
                copies.append(copy)

    def chain_end(phase, h):
        value = own(phase, y, h)
        for direction in range(2):
            if half >= 2 or h == direction:
                ring_copy(phase, direction, half - 1, h).wait_recv()
                value = value + decoded(ring_in[phase, direction, half - 1, h])
        return value

    def start_z(phase):
        z_out[phase] = coded(chain_end(phase, 0))
        copy = pltpu.make_async_remote_copy(
            src_ref=z_out.at[phase], dst_ref=z_in.at[phase],
            send_sem=z_send.at[phase], recv_sem=z_recv.at[phase],
            device_id={"mp": other_z}, device_id_type=MESH,
        )
        copy.start()
        copies.append(copy)
        kept[phase] = chain_end(phase, 1)
        return copy

    wait_phase(back_out, back_send, 0)
    send_back(1)
    receive(0)
    early = half // 2
    for step in range(early):
        ring_step(0, step)
    receive(1)
    for step in range(early, half):
        ring_step(0, step)
        ring_step(1, step - early)
        if step == early:
            sums = [two_sums(0), two_sums(1)]
            mean_out[...] = jnp.concatenate(
                [sums[0][0], sums[1][0], sums[0][1], sums[1][1], jnp.zeros((4, half_rows), F32)], axis=0
            )
            start_sum(1, mean_out, mean_in)
    mean_copy = middle_sum(1, mean_in, mean_zout, mean_zin)
    z_copies = [start_z(0)]
    for step in range(half - early, half):
        ring_step(1, step)
    z_copies.append(start_z(1))

    mean_copy.wait_recv()
    means = (mean_zout[...] + mean_zin[...]) / features
    for phase in range(2):
        z_copies[phase].wait_recv()
        value = kept[phase] + decoded(z_in[phase])
        lines = [value, means[phase : phase + 1], means[phase + 2 : phase + 3]]
        lines.append(jnp.zeros((gvit_v.shape[1] - share - 2, half_rows), F32))
        turn = jnp.transpose(jnp.concatenate(lines, axis=0))
        at = slice(phase * (tile_blocks // 2), (phase + 1) * (tile_blocks // 2))
        turned[at] = turn.reshape(tile_blocks // 2, BLK, gvit_v.shape[1])

    def finish_pair(i, carry):
        at = pl.ds(pl.multiple_of(i * 16, 16), 16)
        pair = []
        for c in range(2):
            j = i * 2 + c
            device = own_phase + j
            phase = lax.rem(device // 2 + me, 2)
            pair.append(turned[phase * (tile_blocks // 2) + 2 * (j // 4) + lax.rem(device, 2)])
        value = jnp.concatenate(pair, axis=0)
        inv = colstat[at, 1:2]
        unit = (hid[at, :] - colstat[at, 0:1]) * inv
        first = value[:, share : share + 1]
        second = value[:, share + 1 : share + 2]
        gvit_v[at, :] = (inv * (value * gain_row - first - unit * second)).astype(BF16)
        return carry

    lax.fori_loop(0, tile_blocks // 2, finish_pair, 0, unroll=2)
    last = pltpu.make_async_copy(gvit_v, gvit_hbm, store_sem.at[2])
    last.start()

    waiting = out_buf.at[pl.ds(0, seq - 1)]
    pltpu.make_async_copy(waiting, waiting, a2a_send).wait()
    wait_phase(back_out, back_send, 1)
    for which, into, copy in ((0, stat_in, stat_copy), (1, mean_in, mean_copy)):
        waiting = into.at[pl.ds(0, ny - 1)]
        pltpu.make_async_copy(waiting, waiting, sum_send.at[which]).wait()
        copy.wait_send()
    for copy in copies:
        copy.wait_send()
    for store in stores:
        store.wait()
    last.wait()


def body(
    vit_hidden,
    vit_gain,
    vit_bias,
    proj_weight,
    text_emb,
    llm_gain,
    cotangent,
    tile_start,
    tile_owner,
):
    seq = lax.axis_size("seq")
    mp = lax.axis_size("mp")
    ny = mp // 2
    rows, features = vit_hidden.shape
    width = proj_weight.shape[1]
    tokens = text_emb.shape[0]
    tile_blocks = rows // BLK
    local_blocks = tokens // BLK
    share = features // mp
    padded = -(-share // 128) * 128

    anywhere = pl.BlockSpec(memory_space=pl.ANY)
    half_width = width // 2
    half = ny // 2
    dma = pltpu.SemaphoreType.DMA
    normed, grad_text, grad_vit = pl.pallas_call(
        functools.partial(kernel, seq, ny, width * mp),
        out_shape=(
            jax.ShapeDtypeStruct((tokens, width), BF16),
            jax.ShapeDtypeStruct((tokens, width), BF16),
            jax.ShapeDtypeStruct((rows, padded), BF16),
        ),
        in_specs=[pl.BlockSpec(memory_space=pltpu.SMEM)] * 2 + [anywhere] * 7,
        out_specs=(anywhere, anywhere, anywhere),
        scratch_shapes=[
            pltpu.VMEM((BLK, 128), jnp.int32),
            pltpu.SMEM((BLK, 128), jnp.int32),
            pltpu.VMEM((1, features), F32),
            pltpu.VMEM((1, features), F32),
            pltpu.VMEM((1, width), F32),
            pltpu.VMEM((rows, features), BF16),
            pltpu.VMEM((features, width), BF16),
            pltpu.VMEM((tokens, width), BF16),
            pltpu.VMEM((tokens, width), BF16),
            pltpu.VMEM((tokens, width), BF16),
            pltpu.VMEM((tokens, width), BF16),
            pltpu.VMEM((rows, padded), BF16),
            pltpu.VMEM((rows + 16, features), BF16),
            pltpu.VMEM((rows, 128), F32),
            pltpu.VMEM((tile_blocks + 2, BLK, width), F32),
            pltpu.VMEM((padded, features), BF16),
            pltpu.VMEM((rows, padded), F32),
            pltpu.VMEM((seq, 16, half_width), BF16),
            pltpu.VMEM((seq, 16, half_width), BF16),
            pltpu.VMEM((local_blocks, BLK, width), F32),
            pltpu.VMEM((local_blocks, BLK, width), F32),
            pltpu.VMEM((local_blocks, BLK, 128), F32),
            pltpu.VMEM((local_blocks, BLK, 128), F32),
            pltpu.VMEM((seq, 16, half_width), BF16),
            pltpu.VMEM((seq // 2, 16, half_width), BF16),
            pltpu.VMEM((seq // 2, 16, half_width), BF16),
            pltpu.VMEM((2, rows // 2, width), BF16),
            pltpu.VMEM((2, rows // 2, width), BF16),
            pltpu.VMEM((2, rows // 2, width), BF16),
            pltpu.VMEM((2, features, rows // 2), F32),
            pltpu.VMEM((2, share, rows // 2), F32),
            pltpu.VMEM((tile_blocks, BLK, padded), F32),
            pltpu.VMEM((BLK, 128), F32),
            pltpu.VMEM((ny, BLK, 128), F32),
            pltpu.VMEM((BLK, 128), F32),
            pltpu.VMEM((BLK, 128), F32),
            pltpu.VMEM((8, rows // 2), F32),
            pltpu.VMEM((ny, 8, rows // 2), F32),
            pltpu.VMEM((8, rows // 2), F32),
            pltpu.VMEM((8, rows // 2), F32),
            pltpu.VMEM((2, 2, half, 2, share + 8, rows // 2), jnp.int16),
            pltpu.VMEM((2, 2, half, 2, share + 8, rows // 2), jnp.int16),
            pltpu.VMEM((2, share + 8, rows // 2), jnp.int16),
            pltpu.VMEM((2, share + 8, rows // 2), jnp.int16),
            dma((8,)),
            dma((3,)),
            dma, dma, dma((2,)), dma((2,)),
            dma((2,)), dma((2,)), dma((2,)), dma((2,)),
            dma((2, 2, half, 2)), dma((2, 2, half, 2)),
            dma((2,)), dma((2,)),
        ],
        compiler_params=pltpu.CompilerParams(
            collective_id=0, has_side_effects=True, vmem_limit_bytes=60 * 2**20
        ),
        name="tiles",
    )(
        tile_start,
        tile_owner,
        vit_hidden,
        vit_gain,
        vit_bias,
        proj_weight,
        text_emb,
        llm_gain,
        cotangent,
    )
    return (normed, grad_text, grad_vit[:, :share])


def solution(mesh):
    in_specs = (
        P("seq", None),
        P(),
        P(),
        P(None, "mp"),
        P("seq", "mp"),
        P("mp"),
        P("seq", "mp"),
        P(),
        P(),
    )
    out_specs = (P("seq", "mp"), P("seq", "mp"), P("seq", "mp"))
    return jax.shard_map(body, mesh=mesh, in_specs=in_specs, out_specs=out_specs, check_vma=False)
```

time: 115 us -> 98.6 us (0.86)
  Pallas kernels: 103 us -> 92.3 us
  local copies, waits for them, and re-layouts: 7.98 us -> 5.39 us
  other arithmetic: 2.16 us -> 0 us
    pallas_call x1, Pallas kernels: 103 us -> 92.3 us  [body(): pl.pallas_call(functools.partial(kernel, seq, ny, width * mp), out_shape=...]
    reshape x2 -> x0, local copies, waits for them, and re-layouts: 1.46 us -> none  [the longest x1 0.73 us: body(): vit_gain.reshape(1, features)]
    unnamed x11 -> x3, local copies, waits for them, and re-layouts: 6.52 us -> 5.39 us
where the time goes in v2:
time: 98.6 us; the launch traced here: 98.4 us
  Pallas kernels  92.3 us (94%)
  local copies, waits for them, and re-layouts  5.39 us (5%)
    pallas_call x1, Pallas kernels, body(): pl.pallas_call(functools.partial(kernel, seq, ny, width * mp), out_shape=...  92.3 us
    unnamed x3, local copies, waits for them, and re-layouts  5.39 us

profile of v2, /device:TPU:8, one launch (start us, length us, event | category | flops | bytes accessed | tf_op | source)
XLA Modules:
  0.0 98.4 jit_solution(13406240088794248157)
XLA Ops:
  0.6 92.3 %tiles.1 = (bf16[512,512]{1,0:T(8,128)(2,1)}, bf16[512,512]{1,0:T(8,128)(2,1)}, bf16[256,256]{1,0:T(8,128)(2,1)}) custom-call(s32[48]{0:T(128)} %starts.1, s32[48]{0:T(128)} %owners.1, bf16[256,3200]{1,0:T(8,128)(2,1)} %vit_hbm.1, f32[3200]{0:T(1024)} %gain_hbm.1, f32[3200]{0:T(1024)} %bias_hbm.1, bf16[3200,512]{1,0:T(8,128)(2,1)} %weight_hbm.1, ...), custom_call_target="tpu_custom_call" | custom-call | tf_op jit(solution)/shard_map/tiles/pallas_call | solution.py:514
  93.0 1.7 %copy.12 = bf16[256,200]{0,1:T(8,128)(2,1)} copy(bf16[256,200]{1,0:T(8,128)(2,1)} %bitcast.1) | data formatting | bytes 204800
  94.6 1.9 %copy.15 = bf16[512,512]{1,0:T(8,128)(2,1)} copy(bf16[512,512]{1,0:T(8,128)(2,1)} %get-tuple-element.15) | data formatting | bytes 1048576
  96.5 1.9 %copy.16 = bf16[512,512]{1,0:T(8,128)(2,1)} copy(bf16[512,512]{1,0:T(8,128)(2,1)} %get-tuple-element.16) | data formatting | bytes 1048576

commit v3 on v2

--- a/solution.py
+++ b/solution.py
@@ -421,7 +421,7 @@
     wait_phase(back_out, back_send, 0)
     send_back(1)
     receive(0)
-    early = half // 2
+    early = max(1, half - 1)
     for step in range(early):
         ring_step(0, step)
     receive(1)

time: 98.6 us -> 104 us (1.055)
  Pallas kernels: 92.3 us -> 97.5 us
    pallas_call x1, Pallas kernels: 92.3 us -> 97.5 us  [body(): pl.pallas_call(functools.partial(kernel, seq, ny, width * mp), out_shape=...]
where the time goes in v3:
time: 104 us
  Pallas kernels  97.5 us (94%)
  local copies, waits for them, and re-layouts  5.39 us (5%)
    pallas_call x1, Pallas kernels, body(): pl.pallas_call(functools.partial(kernel, seq, ny, width * mp), out_shape=...  97.5 us
    unnamed x3, local copies, waits for them, and re-layouts  5.39 us

profile of v3, /device:TPU:8, one launch (start us, length us, event | category | flops | bytes accessed | tf_op | source)
XLA Modules:
  0.0 103.5 jit_solution(8918686596226376163)
XLA Ops:
  0.6 97.5 %tiles.1 = (bf16[512,512]{1,0:T(8,128)(2,1)}, bf16[512,512]{1,0:T(8,128)(2,1)}, bf16[256,256]{1,0:T(8,128)(2,1)}) custom-call(s32[48]{0:T(128)} %starts.1, s32[48]{0:T(128)} %owners.1, bf16[256,3200]{1,0:T(8,128)(2,1)} %vit_hbm.1, f32[3200]{0:T(1024)} %gain_hbm.1, f32[3200]{0:T(1024)} %bias_hbm.1, bf16[3200,512]{1,0:T(8,128)(2,1)} %weight_hbm.1, ...), custom_call_target="tpu_custom_call" | custom-call | tf_op jit(solution)/shard_map/tiles/pallas_call | solution.py:514
  98.1 1.7 %copy.12 = bf16[256,200]{0,1:T(8,128)(2,1)} copy(bf16[256,200]{1,0:T(8,128)(2,1)} %bitcast.1) | data formatting | bytes 204800
  99.8 1.9 %copy.15 = bf16[512,512]{1,0:T(8,128)(2,1)} copy(bf16[512,512]{1,0:T(8,128)(2,1)} %get-tuple-element.15) | data formatting | bytes 1048576
  101.7 1.9 %copy.16 = bf16[512,512]{1,0:T(8,128)(2,1)} copy(bf16[512,512]{1,0:T(8,128)(2,1)} %get-tuple-element.16) | data formatting | bytes 1048576
